TPU v7x, 32 devices: a whole 2x2x4 slice. The times are simulated.
32 devices in a mesh: row: 16 (over z, y, core), col: 2 (over x).
Axes of the slice: x: 2, y: 2, z: 4, core: 2. Of those that a mesh axis runs over, the one named last changes fastest.
Arguments:
- colloc: bfloat16 [2, 1024, 9216], P(None, 'row'), may hold values from -6 to 6
- coefficients: bfloat16 [2, 9216, 512], P(None, 'row'), may hold values from -0.0625 to 0.0625
- occupied: int32 [2], replicated, may hold values from 256 to 512
- offsets: int32 [2, 2], replicated, may hold values from 0 to 1024
Outputs:
- exchange_matrix: bfloat16 [9216, 2, 9216], P('col', None, 'row')
Inputs may be any that keep to these rules, and one draw needn't show every extreme that they name: occupied[s] is the number of occupied orbitals of spin s. offsets[s, k] is the first point of panel k of spin s on the line of 73728 points; both panels lie within the first 1536 points and may intersect.
All inputs are finite; a program needn't handle non-finite values.
Results may differ from a plain program's by a relative error of at most 0.019.
Values may be sent and summed in bfloat16 or wider, within the bound.
A program may use at most 128 MiB of HBM per device.

v0:
```python
import math

import jax
import jax.numpy as jnp
from jax import lax
from jax.sharding import PartitionSpec as P


def point_positions(point_ids, offsets, panel_len):
    first = jnp.where(point_ids[None, :] // panel_len == 0, offsets[:, 0:1], offsets[:, 1:2])
    return (first + point_ids[None, :] % panel_len).astype(jnp.float32)


def local(colloc, coefficients, occupied, offsets):
    row_count = lax.axis_size("row")
    col_count = lax.axis_size("col")
    col_index = lax.axis_index("col")
    spin_count, own_points, basis = colloc.shape
    slots = coefficients.shape[2]
    sub_rows = own_points // col_count
    group_points = row_count * sub_rows
    points = own_points * row_count
    panel_len = points // 2
    screen_len = panel_len // 8
    norm_factor = 1.0 / math.sqrt(points)
    own_rows = lax.dynamic_slice_in_dim(colloc, col_index * sub_rows, sub_rows, 1)
    regrouped = lax.all_to_all(own_rows, "row", split_axis=2, concat_axis=1, tiled=True)
    partial_value = jnp.einsum(
        "spm,smi->spi", regrouped, coefficients, preferred_element_type=jnp.float32
    )
    summed = lax.psum(partial_value, "row")
    occupied_mask = jnp.arange(slots, dtype=jnp.int32)[None, :] < occupied[:, None]
    orbitals_own = jnp.where(occupied_mask[:, None, :], summed, 0.0).astype(jnp.bfloat16)
    orbitals_all, basis_all = (
        lax.all_gather(orbitals_own, "col", axis=1, tiled=True),
        lax.all_gather(regrouped, "col", axis=1, tiled=True),
    )
    local_ids = jnp.arange(group_points, dtype=jnp.int32)
    own_ids = local_ids // sub_rows * own_points + col_index * sub_rows + local_ids % sub_rows
    every_ids = jnp.arange(points, dtype=jnp.int32)
    every_group = every_ids // group_points
    every_rest = every_ids % group_points
    all_ids = every_rest // sub_rows * own_points + every_group * sub_rows + every_rest % sub_rows
    own_positions = point_positions(own_ids, offsets, panel_len)
    all_positions = point_positions(all_ids, offsets, panel_len)
    kernel = 1.0 / (
        1.0 + jnp.abs(own_positions[:, :, None] - all_positions[:, None, :]) / screen_len
    )
    density = jnp.einsum(
        "spi,sqi->spq", orbitals_own, orbitals_all, preferred_element_type=jnp.float32
    )
    mixed_kernel = (kernel * density / slots).astype(jnp.bfloat16)
    weighted = jnp.einsum(
        "spq,sqn->spn", mixed_kernel, basis_all, preferred_element_type=jnp.float32
    ).astype(jnp.bfloat16)
    basis_rows = lax.all_gather(own_rows, "row", axis=1, tiled=True)
    return lax.psum_scatter(
        (
            jnp.einsum("spm,spn->msn", basis_rows, weighted, preferred_element_type=jnp.float32)
            * norm_factor
        ).astype(jnp.bfloat16),
        "col",
        scatter_dimension=0,
        tiled=True,
    )


def solution(mesh):
    placed = (P(None, "row", None), P(None, "row", None), P(), P())
    return jax.shard_map(
        local, mesh=mesh, in_specs=placed, out_specs=P("col", None, "row"), check_vma=False
    )
```

profile of v0, /device:TPU:0, one launch (start us, length us, event | category | flops | bytes accessed | tf_op | source)
XLA Modules:
  0.0 587.7 jit_solution(4174947972321721778)
XLA Ops:
  6.5 0.0 copy-start
  6.5 1.7 copy-done
  8.2 0.1 constant_dynamic-slice_fusion
  8.3 0.0 copy-start.2
  8.3 7.7 %copy.8 = bf16[2,32,9216]{1,0,2:T(2,128)(2,1)} copy(bf16[2,32,9216]{2,1,0:T(8,128)(2,1)S(1)} %constant_dynamic-slice_fusion) | data formatting | bytes 2359296 | tf_op jit(solution)/shard_map/dynamic_slice | solution.py:26
  16.0 0.0 copy-done.2
  16.0 10.8 %reshape.308 = bf16[16,2,18432]{2,1,0:T(2,128)(2,1)} reshape(bf16[9216,2,32]{2,1,0:T(2,128)(2,1)} %bitcast.16) | data formatting | bytes 2359296
  26.9 0.0 copy-start.6
  26.9 7.5 %all-to-all-start = ((bf16[16,2,18432]{2,1,0:T(2,128)(2,1)}), bf16[16,2,18432]{2,1,0:T(2,128)(2,1)S(1)}, u32[]{:S(2)}, u32[]{:S(2)}) async-start(bf16[16,2,18432]{2,1,0:T(2,128)(2,1)} %reshape.308), calls=%async_computation | async-start | bytes 2359296 | tf_op jit(solution)/shard_map/all_to_all | solution.py:27
  34.4 0.0 all-gather.4.cloned.1.call-start
  34.4 0.0 copy-done.6
  34.4 0.1 iota_compare_fusion
  34.5 25.0 %all-to-all-done = bf16[16,2,18432]{2,1,0:T(2,128)(2,1)S(1)} async-done(((bf16[16,2,18432]{2,1,0:T(2,128)(2,1)}), bf16[16,2,18432]{2,1,0:T(2,128)(2,1)S(1)}, u32[]{:S(2)}, u32[]{:S(2)}) %all-to-all-start) | async-done | bytes 1179680 | tf_op jit(solution)/shard_map/all_to_all | solution.py:27
  59.5 3.7 reshape.309
  63.2 0.0 copy-start.4
  63.2 9.5 %copy.9 = bf16[2,32,16,576]{3,1,2,0:T(8,128)(2,1)S(1)} copy(bf16[2,32,16,576]{1,0,3,2:T(2,128)(2,1)} %bitcast.15) | data formatting | bytes 2359296 | tf_op jit(solution)/shard_map/all_to_all | solution.py:27
  72.8 0.0 copy-done.4
  72.8 2.3 fusion.37
  75.1 77.9 %all-reduce.1 = bf16[2,512,512]{2,1,0:T(8,128)(2,1)S(1)} all-reduce(f32[2,512,512]{2,1,0:T(8,128)} %fusion.37), channel_id=1, replica_groups=mesh['row'=16,'col'=2] {'row'}, use_global_device_ids=true, to_apply=%region_0.0 | all-reduce | flops 524288 | bytes 3145728 | tf_op jit(solution)/shard_map/psum | solution.py:31
  153.1 1.2 select_convert_fusion
  154.2 0.0 all-gather.4.cloned.1.call-update
  154.3 0.0 copy-start.5
  154.3 0.0 copy-start.3
  154.3 0.0 all-gather.6.cloned.1.call-start
  154.3 1.4 copy.11
  155.8 0.0 all-gather.6.cloned.1.call-update
  155.8 0.0 all-gather.8.cloned.1.call-start
  155.8 0.7 all-gather.8.cloned.1.call-update
  156.5 0.0 reduce-scatter.2.cloned.1.call-start
  156.6 0.0 copy-done.5
  156.7 0.2 slice_reduce_fusion.1
  156.8 0.1 add_convert_fusion.1
  156.9 0.1 add_convert_fusion
  157.0 27.8 %all-gather.4.cloned.1.call-done = bf16[2,1024,512]{2,1,0:T(8,128)(2,1)} async-done(((bf16[2,512,512]{2,1,0:T(8,128)(2,1)}), bf16[2,1024,512]{2,1,0:T(8,128)(2,1)}) %all-gather.4.cloned.1.call-update) | async-done | bytes 2097168 | tf_op jit(solution)/shard_map/all_gather | solution.py:35
  184.8 37.6 %all-gather.6.cloned.1.call-done = bf16[2,1024,576]{1,2,0:T(8,128)(2,1)} async-done(((bf16[2,512,576]{1,2,0:T(8,128)(2,1)}), bf16[2,1024,576]{1,2,0:T(8,128)(2,1)}) %all-gather.6.cloned.1.call-update) | async-done | bytes 2359312 | tf_op jit(solution)/shard_map/all_gather | solution.py:36
  222.4 0.0 copy-done.3
  222.4 4.9 convolution_convert_fusion
  227.3 95.7 %all-gather.8.cloned.1.call-done = bf16[2,512,9216]{2,1,0:T(8,128)(2,1)} async-done(((bf16[2,32,9216]{2,1,0:T(8,128)(2,1)}), bf16[2,512,9216]{2,1,0:T(8,128)(2,1)}) %all-gather.8.cloned.1.call-update) | async-done | bytes 18874384 | tf_op jit(solution)/shard_map/all_gather | solution.py:56
  323.0 20.9 %fusion = bf16[9216,2,576]{0,2,1:T(8,128)(2,1)} fusion(bf16[2,512,576]{1,2,0:T(8,128)(2,1)S(1)} %convolution_convert_fusion, bf16[2,512,9216]{2,1,0:T(8,128)(2,1)} %all-gather.8.cloned.1.call-done), kind=kOutput, calls=%fused_computation.1 | convolution fusion | flops 10892869632 | bytes 41287680 | tf_op jit(solution)/shard_map/spm,spn->msn/dot_general | solution.py:59
  343.9 0.0 reduce-scatter.2.cloned.1.call-update
  343.9 0.0 copy-start.1
  343.9 237.2 %reduce-scatter.2.cloned.1.call-done = bf16[4608,2,576]{0,2,1:T(8,128)(2,1)} async-done(((bf16[9216,2,576]{0,2,1:T(8,128)(2,1)}), bf16[4608,2,576]{0,2,1:T(8,128)(2,1)}) %reduce-scatter.2.cloned.1.call-update) | async-done | bytes 10616848 | tf_op jit(solution)/shard_map/reduce_scatter | solution.py:57
  581.1 0.0 copy-done.1
  (4 shorter events, 0.1 us)
Async XLA Ops:
  6.5 1.7 copy-start
  8.3 7.7 %copy-start.2 = (bf16[2,32,9216]{2,1,0:T(8,128)(2,1)}, bf16[2,32,9216]{2,1,0:T(8,128)(2,1)S(1)}, u32[]{:S(2)}) copy-start(bf16[2,32,9216]{2,1,0:T(8,128)(2,1)S(1)} %constant_dynamic-slice_fusion) | copy-start | bytes 3538948
  26.9 7.6 %copy-start.6 = (s32[2]{0:T(128)S(1)}, s32[2]{0:T(128)}, u32[]{:S(2)}) copy-start(s32[2]{0:T(128)} %param.6) | copy-start | bytes 28
  26.9 32.7 %all-to-all-start = ((bf16[16,2,18432]{2,1,0:T(2,128)(2,1)}), bf16[16,2,18432]{2,1,0:T(2,128)(2,1)S(1)}, u32[]{:S(2)}, u32[]{:S(2)}) async-start(bf16[16,2,18432]{2,1,0:T(2,128)(2,1)} %reshape.308), calls=%async_computation | async-start | bytes 2359296 | tf_op jit(solution)/shard_map/all_to_all | solution.py:27
  34.4 150.4 %all-gather.4.cloned.1.call-start = ((), (), s32[]{:S(2)}) async-start(), calls=%async_computation.2 | async-start | bytes 3145728 | tf_op jit(solution)/shard_map/all_gather | solution.py:35
  63.2 9.6 %copy-start.4 = (bf16[2,576,512]{2,1,0:T(8,128)(2,1)S(1)}, bf16[2,576,512]{2,1,0:T(8,128)(2,1)}, u32[]{:S(2)}) copy-start(bf16[2,576,512]{2,1,0:T(8,128)(2,1)} %param.5) | copy-start | bytes 3538948
  154.3 2.4 copy-start.5
  154.3 68.2 %copy-start.3 = (bf16[2,512,512]{2,1,0:T(8,128)(2,1)S(1)}, bf16[2,512,512]{2,1,0:T(8,128)(2,1)}, u32[]{:S(2)}) copy-start(bf16[2,512,512]{2,1,0:T(8,128)(2,1)} %select_convert_fusion) | copy-start | bytes 3145732
  154.3 68.2 %all-gather.6.cloned.1.call-start = ((), (), s32[]{:S(2)}) async-start(), calls=%async_computation.3 | async-start | bytes 3538944 | tf_op jit(solution)/shard_map/all_gather | solution.py:36
  155.8 167.2 %all-gather.8.cloned.1.call-start = ((), (), s32[]{:S(2)}) async-start(), calls=%async_computation.4 | async-start | bytes 20054016 | tf_op jit(solution)/shard_map/all_gather | solution.py:56
  156.5 424.6 %reduce-scatter.2.cloned.1.call-start = ((), (), s32[]{:S(2)}) async-start(), calls=%async_computation.5 | async-start | bytes 31850496 | tf_op jit(solution)/shard_map/reduce_scatter | solution.py:57
  343.9 237.2 %copy-start.1 = (bf16[2,64,9216]{2,1,0:T(8,128)(2,1)S(1)}, bf16[2,64,9216]{2,1,0:T(8,128)(2,1)}, u32[]{:S(2)}) copy-start(bf16[2,64,9216]{2,1,0:T(8,128)(2,1)} %param.4) | copy-start | bytes 7077892
Sparse Core Ops, SparseCore 0:
  154.4 30.3 all-gather.3
  186.3 36.0 all-gather.5
  224.0 98.9 all-gather.7
  344.1 237.0 reduce-scatter.1
where the time goes:
time: 588 us
  waiting for transfers between devices  424 us (72%)
  blocking collectives  77.9 us (13%)
  local copies, waits for them, and re-layouts  35.2 us (6%)
  matrix products  28.1 us (5%)
  between operations  13.2 us (2%)
  starting transfers between devices  7.68 us (1%)
    reduce_scatter x1, waiting for transfers between devices, local(): lax.psum_scatter((jnp.einsum('spm,spn->msn', basis_rows, weighted, prefer...  237 us
    all_gather x1, waiting for transfers between devices, local(): basis_rows = lax.all_gather(own_rows, 'row', axis=1, tiled=True)  95.7 us
    psum x1, blocking collectives, local(): summed = lax.psum(partial_value, 'row')  77.9 us
    all_gather x1, waiting for transfers between devices, local(): lax.all_gather(regrouped, 'col', axis=1, tiled=True)  37.6 us
    all_gather x1, waiting for transfers between devices, local(): lax.all_gather(orbitals_own, 'col', axis=1, tiled=True)  27.8 us
    all_to_all x1, waiting for transfers between devices, local(): lax.all_to_all(own_rows, 'row', split_axis=2, concat_axis=1, tiled=True)  25 us
    dot_general x1, matrix products, local(): jnp.einsum('spm,spn->msn', basis_rows, weighted, preferred_element_type=j...  20.9 us
    unnamed x16, local copies, waits for them, and re-layouts  16.2 us
  transfers between devices with their start and end apart: 5, of which 5 were waited for; matrix products, arithmetic and copies ran while one was open for 1% of the time, Pallas kernels for 0%

commit v1 on v0

v1 whole, which is shorter than its diff:
```python
import math

import jax
import jax.numpy as jnp
from jax import lax
from jax.sharding import PartitionSpec as P


def positions_of(offsets, points, panel_len):
    ids = jnp.arange(points, dtype=jnp.int32)
    first = jnp.where(ids[None, :] // panel_len == 0, offsets[:, 0:1], offsets[:, 1:2])
    return (first + ids[None, :] % panel_len).astype(jnp.float32)


def local(colloc, coefficients, occupied, offsets):
    rows = lax.axis_size("row")
    cols = lax.axis_size("col")
    row = lax.axis_index("row")
    col = lax.axis_index("col")
    spins, own_points, basis = colloc.shape
    depth, slots = coefficients.shape[1:]
    points = own_points * rows
    panel_len = points // 2
    screen_len = panel_len // 8
    share = basis // cols
    part = depth // cols
    own_coefficients = lax.dynamic_slice_in_dim(coefficients, col * part, part, 1)
    coefficient_share = lax.all_gather(own_coefficients, "row", axis=1, tiled=True)
    own_share = lax.dynamic_slice_in_dim(colloc, col * share, share, 2)
    basis_share = lax.all_gather(own_share, "row", axis=1, tiled=True)
    cut = colloc.reshape(spins, own_points, rows, cols, part)
    cut = lax.dynamic_index_in_dim(cut, col, 3, keepdims=False).reshape(spins, own_points, rows * part)
    partial_value = jnp.einsum("spm,smi->spi", cut, coefficient_share, preferred_element_type=jnp.float32)
    summed = lax.psum(partial_value, "col")
    occupied_mask = jnp.arange(slots, dtype=jnp.int32)[None, :] < occupied[:, None]
    own_orbitals = jnp.where(occupied_mask[:, None, :], summed, 0.0).astype(jnp.bfloat16)
    orbitals = lax.all_gather(own_orbitals, "row", axis=1, tiled=True)
    place = positions_of(offsets, points, panel_len)
    kernel = 1.0 / (1.0 + jnp.abs(place[:, :, None] - place[:, None, :]) / screen_len)
    density = jnp.einsum("spi,sqi->spq", orbitals, orbitals, preferred_element_type=jnp.float32)
    mixed_kernel = (kernel * density / slots).astype(jnp.bfloat16)
    per_col = rows // cols
    own_window = lax.dynamic_slice_in_dim(basis_share, row % per_col * depth, depth, 2)
    window = lax.psum(jnp.where(row // per_col == col, own_window, jnp.bfloat16(0)), "col")
    weighted = jnp.einsum("spq,sqn->spn", mixed_kernel, window, preferred_element_type=jnp.float32)
    weighted = weighted.astype(jnp.bfloat16)
    result = jnp.einsum("spm,spn->msn", basis_share, weighted, preferred_element_type=jnp.float32)
    return (result * (1.0 / math.sqrt(points))).astype(jnp.bfloat16)


def solution(mesh):
    placed = (P(None, "row", None), P(None, "row", None), P(), P())
    return jax.shard_map(
        local, mesh=mesh, in_specs=placed, out_specs=P("col", None, "row"), check_vma=False
    )
```

time: 588 us -> 346 us (0.59)
  waiting for transfers between devices: 424 us -> 253 us
  blocking collectives: 77.9 us -> 12.2 us
  starting transfers between devices: 7.68 us -> 0.13 us
  local copies, waits for them, and re-layouts: 35.2 us -> 27.8 us
    reduce_scatter x1 -> x0, waiting for transfers between devices: 237 us -> none  [local(): lax.psum_scatter((jnp.einsum('spm,spn->msn', basis_rows, weighted, prefer...]
    psum x0 -> x1, waiting for transfers between devices: none -> 75.3 us  [local(): lax.psum(jnp.where(row // per_col == col, own_window, jnp.bfloat16(0)), '...]
    psum x1, blocking collectives: 77.9 us -> 12.2 us  [local(): summed = lax.psum(partial_value, 'col')]
    all_to_all x1 -> x0, waiting for transfers between devices: 25 us -> none  [local(): lax.all_to_all(own_rows, 'row', split_axis=2, concat_axis=1, tiled=True)]
    all_gather x3, waiting for transfers between devices: 161 us -> 178 us  [the longest x1 80.2 us: local(): basis_share = lax.all_gather(own_share, 'row', axis=1, tiled=True)]
    unnamed x16 -> x8, local copies, waits for them, and re-layouts: 16.2 us -> 1.91 us
    all_to_all x2 -> x0, local copies, waits for them, and re-layouts: 11 us -> none  [local(): lax.all_to_all(own_rows, 'row', split_axis=2, concat_axis=1, tiled=True)]
    reshape x0 -> x2, local copies, waits for them, and re-layouts: none -> 9.39 us  [the longest x1 6.42 us: local(): cut = colloc.reshape(spins, own_points, rows, cols, part)]
  transfers between devices with their start and end apart: 5 -> 4, of which waited for: 5 -> 4; matrix products, arithmetic and copies ran while one was open for 1% -> 11% of each run, Pallas kernels for 0% -> 0%
where the time goes in v1:
time: 346 us; the launch traced here: 345 us
  waiting for transfers between devices  253 us (73%)
  matrix products  32.9 us (10%)
  local copies, waits for them, and re-layouts  27.8 us (8%)
  between operations  13.2 us (4%)
  blocking collectives  12.2 us (4%)
  other arithmetic  5.79 us (2%)
    all_gather x1, waiting for transfers between devices, local(): basis_share = lax.all_gather(own_share, 'row', axis=1, tiled=True)  80.2 us
    psum x1, waiting for transfers between devices, local(): lax.psum(jnp.where(row // per_col == col, own_window, jnp.bfloat16(0)), '...  75.3 us
    all_gather x1, waiting for transfers between devices, local(): lax.all_gather(own_coefficients, 'row', axis=1, tiled=True)  60.1 us
    all_gather x1, waiting for transfers between devices, local(): orbitals = lax.all_gather(own_orbitals, 'row', axis=1, tiled=True)  37.8 us
    dot_general x1, matrix products, local(): jnp.einsum('spm,spn->msn', basis_share, weighted, preferred_element_type=...  19.7 us
    dynamic_slice x1, local copies, waits for them, and re-layouts, local(): lax.dynamic_index_in_dim(cut, col, 3, keepdims=False)  13.1 us
    psum x1, blocking collectives, local(): summed = lax.psum(partial_value, 'col')  12.2 us
    dot_general x1, matrix products, local(): jnp.einsum('spq,sqn->spn', mixed_kernel, window, preferred_element_type=j...  7.69 us
  transfers between devices with their start and end apart: 4, of which 4 were waited for; matrix products, arithmetic and copies ran while one was open for 11% of the time, Pallas kernels for 0%

profile of v1, /device:TPU:0, one launch (start us, length us, event | category | flops | bytes accessed | tf_op | source)
XLA Modules:
  0.0 345.4 jit_solution(5235212947641260749)
XLA Ops:
  6.5 0.0 copy-start
  6.5 0.0 all-gather.4.cloned.1.call-start
  6.5 1.3 copy-done
  7.8 0.0 copy-start.1
  7.8 0.8 constant_dynamic-slice_fusion.1
  8.7 0.0 all-gather.4.cloned.1.call-update
  8.7 0.0 all-gather.8.cloned.1.call-start
  8.7 2.4 constant_dynamic-slice_fusion
  11.1 0.0 all-gather.8.cloned.1.call-update
  11.1 0.0 all-gather.6.cloned.1.call-start
  11.2 0.0 copy-done.1
  11.2 6.4 %reshape.186 = bf16[2,64,16,2,288]{4,3,2,1,0:T(2,128)(2,1)} reshape(bf16[2,64,9216]{2,1,0:T(8,128)(2,1)S(1)} %copy-done.1) | data formatting | bytes 4718592 | tf_op jit(solution)/shard_map/reshape | solution.py:31
  17.6 0.0 copy-start.3
  17.6 13.1 %dynamic-slice_reduce_fusion = bf16[2,64,16,288]{3,2,1,0:T(8,128)(2,1)} fusion(bf16[2,64,16,2,288]{4,3,2,1,0:T(2,128)(2,1)} %reshape.186, s32[]{:T(128)S(6)} %select_n.72), kind=kLoop, calls=%fused_computation.4 | loop fusion | bytes 2359300 | tf_op jit(solution)/shard_map/jit(dynamic_index_in_dim)/dynamic_slice | solution.py:32
  30.7 3.0 reshape.187
  33.7 0.0 copy-done.3
  33.7 0.1 iota_compare_fusion
  33.8 60.1 %all-gather.4.cloned.1.call-done = bf16[2,4608,512]{2,1,0:T(8,128)(2,1)} async-done(((bf16[2,288,512]{2,1,0:T(8,128)(2,1)}), bf16[2,4608,512]{2,1,0:T(8,128)(2,1)}) %all-gather.4.cloned.1.call-update) | async-done | bytes 9437200 | tf_op jit(solution)/shard_map/all_gather | solution.py:28
  93.8 5.5 %fusion.16 = f32[2,64,512]{2,1,0:T(8,128)S(1)} fusion(bf16[2,64,4608]{2,1,0:T(8,128)(2,1)S(1)} %reshape.187, bf16[2,4608,512]{2,1,0:T(8,128)(2,1)} %all-gather.4.cloned.1.call-done), kind=kOutput, calls=%fused_computation.30 | convolution fusion | flops 603979776 | bytes 10878976 | tf_op jit(solution)/shard_map/spm,smi->spi/dot_general | solution.py:33
  99.3 12.2 %all-reduce.4 = bf16[2,64,512]{2,1,0:T(8,128)(2,1)S(1)} all-reduce(f32[2,64,512]{2,1,0:T(8,128)S(1)} %fusion.16), channel_id=1, replica_groups=mesh['row'=16,'col'=2] {'col'}, use_global_device_ids=true, to_apply=%region_0.1 | all-reduce | flops 65536 | bytes 393216 | tf_op jit(solution)/shard_map/psum | solution.py:34
  111.5 0.7 select_convert_fusion
  112.2 0.0 all-gather.6.cloned.1.call-update
  112.2 0.0 all-reduce.3.cloned.1.call-start
  112.3 80.2 %all-gather.8.cloned.1.call-done = bf16[2,1024,4608]{2,1,0:T(8,128)(2,1)} async-done(((bf16[2,64,4608]{2,1,0:T(8,128)(2,1)}), bf16[2,1024,4608]{2,1,0:T(8,128)(2,1)}) %all-gather.8.cloned.1.call-update) | async-done | bytes 18874384 | tf_op jit(solution)/shard_map/all_gather | solution.py:30
  192.5 4.9 %dynamic-slice_select_fusion = bf16[2,1024,576]{2,1,0:T(8,128)(2,1)} fusion(bf16[2,1024,4608]{2,1,0:T(8,128)(2,1)} %all-gather.8.cloned.1.call-done, s32[]{:T(128)S(6)} %select_n.79, pred[]{:T(512)S(6)} %eq.17), kind=kLoop, calls=%fused_computation.5 | loop fusion | flops 1179648 | bytes 4718597 | tf_op jit(solution)/shard_map/jit(_where)/select_n | solution.py:44
  197.5 0.0 copy-start.2
  197.5 0.0 all-reduce.3.cloned.1.call-update
  197.5 0.6 copy-done.2
  198.1 0.2 slice_reduce_fusion.1
  198.3 0.1 add_convert_fusion
  198.4 37.8 %all-gather.6.cloned.1.call-done = bf16[2,1024,512]{2,1,0:T(8,128)(2,1)} async-done(((bf16[2,64,512]{2,1,0:T(8,128)(2,1)}), bf16[2,1024,512]{2,1,0:T(8,128)(2,1)}) %all-gather.6.cloned.1.call-update) | async-done | bytes 2097168 | tf_op jit(solution)/shard_map/all_gather | solution.py:37
  236.2 75.3 %all-reduce.3.cloned.1.call-done = bf16[2,1024,576]{2,1,0:T(8,128)(2,1)} async-done(((bf16[2,1024,576]{2,1,0:T(8,128)(2,1)}), bf16[2,1024,576]{2,1,0:T(8,128)(2,1)}) %all-reduce.3.cloned.1.call-update) | async-done | bytes 2359312 | tf_op jit(solution)/shard_map/psum | solution.py:44
  311.5 7.7 %fusion.1 = bf16[2,1024,576]{1,2,0:T(8,128)(2,1)S(1)} fusion(bf16[2,1024,576]{2,1,0:T(8,128)(2,1)} %all-reduce.3.cloned.1.call-done, f32[2,1024]{1,0:T(2,128)S(1)} %add_convert_fusion, bf16[2,1024,512]{2,1,0:T(8,128)(2,1)} %all-gather.6.cloned.1.call-done), kind=kOutput, calls=%fused_computation.3 | convolution fusion | flops 4580179968 | bytes 6823936 | tf_op jit(solution)/shard_map/spq,sqn->spn/dot_general | solution.py:45
  319.2 19.7 %fusion = bf16[4608,2,576]{0,2,1:T(8,128)(2,1)} fusion(bf16[2,1024,4608]{2,1,0:T(8,128)(2,1)} %all-gather.8.cloned.1.call-done, bf16[2,1024,576]{1,2,0:T(8,128)(2,1)S(1)} %fusion.1), kind=kOutput, calls=%fused_computation.1 | convolution fusion | flops 10882252800 | bytes 31850496 | tf_op jit(solution)/shard_map/spm,spn->msn/dot_general | solution.py:47
  (2 shorter events, 0.0 us)
Async XLA Ops:
  6.5 1.3 copy-start
  6.5 87.3 %all-gather.4.cloned.1.call-start = ((), (), s32[]{:S(2)}) async-start(), calls=%async_computation | async-start | bytes 10027008 | tf_op jit(solution)/shard_map/all_gather | solution.py:28
  7.8 3.4 copy-start.1
  8.7 183.8 %all-gather.8.cloned.1.call-start = ((), (), s32[]{:S(2)}) async-start(), calls=%async_computation.2 | async-start | bytes 20054016 | tf_op jit(solution)/shard_map/all_gather | solution.py:30
  11.1 225.0 %all-gather.6.cloned.1.call-start = ((), (), s32[]{:S(2)}) async-start(), calls=%async_computation.1 | async-start | bytes 2228224 | tf_op jit(solution)/shard_map/all_gather | solution.py:37
  17.6 16.1 %copy-start.3 = (s32[2]{0:T(128)S(1)}, s32[2]{0:T(128)}, u32[]{:S(2)}) copy-start(s32[2]{0:T(128)} %param.6) | copy-start | bytes 28
  112.2 199.2 %all-reduce.3.cloned.1.call-start = ((), (), s32[]{:S(2)}) async-start(), calls=%async_computation.3 | async-start | bytes 5242880 | tf_op jit(solution)/shard_map/psum | solution.py:44
  197.5 0.7 copy-start.2
Sparse Core Ops, SparseCore 0:
  9.6 84.1 all-gather.3
  95.4 97.0 all-gather.7
  194.7 41.4 all-gather.5
  238.3 73.1 all-reduce.2

commit v2 on v1

v2 whole, which is shorter than its diff:
```python
import functools
import math

import jax
import jax.numpy as jnp
from jax import lax
from jax.experimental import pallas as pl
from jax.experimental.pallas import tpu as pltpu
from jax.sharding import PartitionSpec as P

MESH = pl.DeviceIdType.MESH
LANES = 128


def positions_of(offsets, points, panel_len):
    ids = jnp.arange(points, dtype=jnp.int32)
    first = jnp.where(ids[None, :] // panel_len == 0, offsets[:, 0:1], offsets[:, 1:2])
    return (first + ids[None, :] % panel_len).astype(jnp.float32)


def window_lanes(depth):
    over = LANES - math.gcd(depth, LANES)
    return -(-(depth + over) // LANES) * LANES


class Ring:
    def __init__(self, place, own, piece, ring_send, ring_recv, pair_send, pair_recv):
        self.place, self.own, self.piece = place, own, piece
        self.ring_send, self.ring_recv = ring_send, ring_recv
        self.pair_send, self.pair_recv = pair_send, pair_recv

    def origin(self, way, step, core):
        chips = self.place["chips"]
        back = -step if way == 0 else step
        return self.place["chip_at"](lax.rem(self.place["position"] + back + chips, chips)) * 2 + core

    def source(self, way, step):
        return self.own(way) if step == 0 else self.piece(way, self.origin(way, step, self.place["core"]))

    def hop(self, way, step):
        target = self.place["next"] if way == 0 else self.place["previous"]
        return pltpu.make_async_remote_copy(
            src_ref=self.source(way, step),
            dst_ref=self.piece(way, self.origin(way, step, self.place["core"])),
            send_sem=self.ring_send.at[way, step % 2],
            recv_sem=self.ring_recv.at[way, step],
            device_id=(target, self.place["col"]),
            device_id_type=MESH,
        )

    def landed(self, way, step):
        return pltpu.make_async_remote_copy(
            src_ref=self.source(way, step),
            dst_ref=self.piece(way, self.origin(way, step + 1, self.place["core"])),
            send_sem=self.ring_send.at[way, step % 2],
            recv_sem=self.ring_recv.at[way, step],
            device_id=(self.place["next"], self.place["col"]),
            device_id_type=MESH,
        )

    def hand(self, way, step):
        return pltpu.make_async_remote_copy(
            src_ref=self.source(way, step),
            dst_ref=self.piece(way, self.origin(way, step, self.place["core"])),
            send_sem=self.pair_send.at[way, step % 2],
            recv_sem=self.pair_recv.at[way, step],
            device_id=(self.place["sibling"], self.place["col"]),
            device_id_type=MESH,
        )

    def handed(self, way, step):
        return pltpu.make_async_remote_copy(
            src_ref=self.source(way, step),
            dst_ref=self.piece(way, self.origin(way, step, 1 - self.place["core"])),
            send_sem=self.pair_send.at[way, step % 2],
            recv_sem=self.pair_recv.at[way, step],
            device_id=(self.place["sibling"], self.place["col"]),
            device_id_type=MESH,
        )

    def begin(self):
        for way in (0, 1):
            self.hop(way, 0).start()
        for way in (0, 1):
            self.hand(way, 0).start()

    def advance(self, step):
        chips = self.place["chips"]
        for way in (0, 1):
            self.landed(way, step).wait_recv()
            if step + 1 < chips - 1:
                if step >= 1:
                    self.hop(way, step - 1).wait_send()
                self.hop(way, step + 1).start()
            if step >= 1:
                self.hand(way, step - 1).wait_send()
            self.hand(way, step + 1).start()

    def finish_sends(self):
        chips = self.place["chips"]
        for way in (0, 1):
            for step in range(max(chips - 3, 0), chips - 1):
                self.hop(way, step).wait_send()
            for step in range(chips - 2, chips):
                self.hand(way, step).wait_send()


def transfers(
    rows, cols, slot_blocks, colloc, coefficients, basis_share, window, orbitals,
    all_coefficients, own_colloc, own_orbitals, total, local_sem,
    c_rs, c_rr, c_ps, c_pr, b_rs, b_rr, b_ps, b_pr, o_rs, o_rr, o_ps, o_pr,
    x_send, x_recv, w_local, y_send, y_recv,
):
    row, col = lax.axis_index("row"), lax.axis_index("col")
    spins, own_points, basis = colloc.shape
    depth, slots = coefficients.shape[1:]
    share = basis // cols
    width = window.shape[2]
    per_col = rows // cols
    chips = rows // 2
    side = chips // 2
    core, chip = row % 2, row // 2

    def chip_at(position):
        high = position // side
        return (position + high * (chips - 1 - 2 * position)) * 2 + high

    position = chip // 2 + (chip % 2) * (chips - 1 - 2 * (chip // 2))
    place = dict(
        chips=chips, chip_at=chip_at, position=position, core=core, col=col,
        next=chip_at(lax.rem(position + 1, chips)) * 2 + core,
        previous=chip_at(lax.rem(position + chips - 1, chips)) * 2 + core,
        sibling=chip * 2 + 1 - core,
    )
    other_cols = [lax.rem(col + shift, cols) for shift in range(1, cols)]
    spin, block = col % spins, col // spins
    block_len = slots // slot_blocks
    block_lanes = pl.ds(pl.multiple_of(block * block_len, LANES), block_len)
    share_start = pl.multiple_of(col * share, LANES)
    half = depth // 2

    barrier = pltpu.get_barrier_semaphore()
    for other in (place["next"], place["previous"], place["sibling"]):
        pl.semaphore_signal(barrier, inc=1, device_id=(other, col), device_id_type=MESH)
    for other in other_cols:
        pl.semaphore_signal(barrier, inc=1, device_id=(row, other), device_id_type=MESH)
    pl.semaphore_wait(barrier, 3 + len(other_cols))

    def point_rows(at):
        return pl.ds(pl.multiple_of(at * own_points, own_points), own_points)

    coefficient_ring = Ring(
        place,
        lambda way: coefficients.at[spin, pl.ds(way * half, half), block_lanes],
        lambda way, at: all_coefficients.at[pl.ds(pl.multiple_of(at * depth + way * half, 16), half), :],
        c_rs, c_rr, c_ps, c_pr,
    )
    basis_ring = Ring(
        place,
        lambda way: colloc.at[way, :, pl.ds(share_start, share)],
        lambda way, at: basis_share.at[way, point_rows(at), :],
        b_rs, b_rr, b_ps, b_pr,
    )
    orbital_ring = Ring(
        place,
        lambda way: own_orbitals.at[way],
        lambda way, at: orbitals.at[way, point_rows(at), :],
        o_rs, o_rr, o_ps, o_pr,
    )

    coefficient_ring.begin()
    basis_ring.begin()
    local = [
        pltpu.make_async_copy(
            coefficients.at[spin, :, block_lanes],
            all_coefficients.at[pl.ds(pl.multiple_of(row * depth, 16), depth), :],
            local_sem.at[0],
        ),
        pltpu.make_async_copy(colloc.at[spin], own_colloc, local_sem.at[1]),
        pltpu.make_async_copy(
            colloc.at[:, :, pl.ds(share_start, share)],
            basis_share.at[:, point_rows(row), :],
            local_sem.at[2],
        ),
    ]
    for copy in local:
        copy.start()

    owner = row // per_col == col
    first_lane = pl.multiple_of((row % per_col) * depth // LANES * LANES, LANES)

    def window_piece(way, step, at_core):
        at = basis_ring.origin(way, step, at_core)
        relation = at_core_index(at_core)
        source = basis_share.at[way, point_rows(at), pl.ds(first_lane, width)]
        target = window.at[way, point_rows(at), :]
        here = pltpu.make_async_copy(source, target, w_local.at[relation, way, step % 2])
        away = [
            pltpu.make_async_remote_copy(
                src_ref=source, dst_ref=target,
                send_sem=x_send.at[n, relation, way, step % 2],
                recv_sem=x_recv.at[relation, way, step],
                device_id=(row, other), device_id_type=MESH,
            )
            for n, other in enumerate(other_cols)
        ]
        return here, away

    def at_core_index(at_core):
        return 0 if at_core is core else 1

    other_core = 1 - core

    def start_window(step, at_core):
        @pl.when(owner)
        def _():
            for way in (0, 1):
                if step >= 2:
                    here, away = window_piece(way, step - 2, at_core)
                    here.wait()
                    for copy in away:
                        copy.wait_send()
                here, away = window_piece(way, step, at_core)
                for copy in away:
                    copy.start()
                here.start()

    def wait_handed(ring, step):
        for way in (0, 1):
            ring.handed(way, step).wait_recv()

    def basis_step(step):
        basis_ring.advance(step)
        if step == 0:
            local[2].wait()
            start_window(0, core)
        start_window(step + 1, core)
        wait_handed(basis_ring, step)
        start_window(step, other_core)

    last = chips - 1
    done = 0
    early = max(last * 2 // 7, 1)
    for step in range(last):
        coefficient_ring.advance(step)
        if (step + 1) * early // last > done:
            basis_step(done)
            done += 1
    for step in range(chips):
        wait_handed(coefficient_ring, step)
    local[0].wait()
    local[1].wait()

    total[...] = jnp.zeros_like(total)
    chunk = 9 * LANES if basis % (9 * LANES) == 0 else LANES

    @pl.loop(0, basis // chunk)
    def _(i):
        at = pl.ds(pl.multiple_of(i * chunk, chunk), chunk)
        total[...] += jnp.dot(own_colloc[:, at], all_coefficients[at, :], preferred_element_type=jnp.float32)

    own_orbitals[spin, :, block_lanes] = total[...].astype(jnp.bfloat16)
    swaps = [
        pltpu.make_async_remote_copy(
            src_ref=own_orbitals.at[spin, :, block_lanes],
            dst_ref=own_orbitals.at[spin, :, block_lanes],
            send_sem=y_send.at[n], recv_sem=y_recv.at[n],
            device_id=(row, other), device_id_type=MESH,
        )
        for n, other in enumerate(other_cols)
    ]
    for copy in swaps:
        copy.start()
    for n in range(cols - 1):
        came = lax.rem(col + cols - 1 - n, cols)
        lanes = pl.ds(pl.multiple_of(came // spins * block_len, LANES), block_len)
        pltpu.make_async_remote_copy(
            src_ref=own_orbitals.at[spin, :, block_lanes],
            dst_ref=own_orbitals.at[came % spins, :, lanes],
            send_sem=y_send.at[n], recv_sem=y_recv.at[n],
            device_id=(row, came), device_id_type=MESH,
        ).wait_recv()
    orbital_ring.begin()
    own_out = pltpu.make_async_copy(own_orbitals, orbitals.at[:, point_rows(row), :], local_sem.at[3])
    own_out.start()
    left, sent = last - done, 0
    for n in range(left):
        basis_step(done)
        done += 1
        while sent < last and sent < -(-(n + 1) * last // max(left - 1, 1)):
            orbital_ring.advance(sent)
            sent += 1
    wait_handed(basis_ring, last)
    start_window(last, other_core)
    for step in range(chips):
        wait_handed(orbital_ring, step)
    own_out.wait()
    for copy in swaps:
        copy.wait_send()
    for ring in (coefficient_ring, basis_ring, orbital_ring):
        ring.finish_sends()

    @pl.when(owner)
    def _():
        for at_core in (core, other_core):
            for step in (last - 1, last):
                for way in (0, 1):
                    here, away = window_piece(way, step, at_core)
                    here.wait()
                    for copy in away:
                        copy.wait_send()

    @pl.when(jnp.logical_not(owner))
    def _():
        for at_core in (core, other_core):
            for step in range(chips):
                for way in (0, 1):
                    window_piece(way, step, at_core)[1][0].wait_recv()


def gathered(colloc, coefficients, rows, cols):
    spins, own_points, basis = colloc.shape
    depth, slots = coefficients.shape[1:]
    points, share, chips = own_points * rows, basis // cols, rows // 2
    slot_blocks = cols // spins
    block_len = slots // slot_blocks
    dma = pltpu.SemaphoreType.DMA
    ring = [dma((2, 2)), dma((2, chips - 1)), dma((2, 2)), dma((2, chips))]
    anywhere = pl.BlockSpec(memory_space=pl.ANY)
    return pl.pallas_call(
        functools.partial(transfers, rows, cols, slot_blocks),
        out_shape=(
            jax.ShapeDtypeStruct((spins, points, share), colloc.dtype),
            jax.ShapeDtypeStruct((spins, points, window_lanes(depth)), colloc.dtype),
            jax.ShapeDtypeStruct((spins, points, slots), colloc.dtype),
        ),
        in_specs=[anywhere] * 2,
        out_specs=(anywhere,) * 3,
        scratch_shapes=[
            pltpu.VMEM((basis, block_len), colloc.dtype),
            pltpu.VMEM((own_points, basis), colloc.dtype),
            pltpu.VMEM((spins, own_points, slots), colloc.dtype),
            pltpu.VMEM((own_points, block_len), jnp.float32),
            dma((4,)),
            *ring, *ring, *ring,
            dma((cols - 1, 2, 2, 2)), dma((2, 2, chips)), dma((2, 2, 2)),
            dma((cols - 1,)), dma((cols - 1,)),
        ],
        compiler_params=pltpu.CompilerParams(
            collective_id=0, has_side_effects=True, vmem_limit_bytes=24 * 2**20
        ),
    )(colloc, coefficients)


def local(colloc, coefficients, occupied, offsets):
    rows = lax.axis_size("row")
    cols = lax.axis_size("col")
    row = lax.axis_index("row")
    spins, own_points, basis = colloc.shape
    depth, slots = coefficients.shape[1:]
    points = own_points * rows
    panel_len = points // 2
    screen_len = panel_len // 8
    basis_share, window, orbitals = gathered(colloc, coefficients, rows, cols)
    occupied_mask = jnp.arange(slots, dtype=jnp.int32)[None, :] < occupied[:, None]
    orbitals = jnp.where(occupied_mask[:, None, :], orbitals, jnp.bfloat16(0))
    place = positions_of(offsets, points, panel_len)
    kernel = 1.0 / (1.0 + jnp.abs(place[:, :, None] - place[:, None, :]) / screen_len)
    density = jnp.einsum("spi,sqi->spq", orbitals, orbitals, preferred_element_type=jnp.float32)
    mixed_kernel = (kernel * density / slots).astype(jnp.bfloat16)
    weighted = jnp.einsum("spq,sqn->spn", mixed_kernel, window, preferred_element_type=jnp.float32)
    weighted = lax.dynamic_slice_in_dim(weighted.astype(jnp.bfloat16), row * depth % LANES, depth, 2)
    result = jnp.einsum("spm,spn->msn", basis_share, weighted, preferred_element_type=jnp.float32)
    return (result * (1.0 / math.sqrt(points))).astype(jnp.bfloat16)


def solution(mesh):
    placed = (P(None, "row", None), P(None, "row", None), P(), P())
    return jax.shard_map(
        local, mesh=mesh, in_specs=placed, out_specs=P("col", None, "row"), check_vma=False
    )
```

time: 346 us -> 203 us (0.59)
  waiting for transfers between devices: 253 us -> 0 us
  Pallas kernels: 0 us -> 162 us
  local copies, waits for them, and re-layouts: 27.8 us -> 11.7 us
  between operations: 13.2 us -> 0.02 us
  blocking collectives: 12.2 us -> 0 us
  matrix products: 32.9 us -> 27.1 us
  other arithmetic: 5.79 us -> 0.82 us
    all_gather x3 -> x0, waiting for transfers between devices: 178 us -> none  [the longest x1 80.2 us: local(): basis_share = lax.all_gather(own_share, 'row', axis=1, tiled=True)]
    pallas_call x0 -> x1, Pallas kernels: none -> 162 us  [gathered(): pl.pallas_call(functools.partial(transfers, rows, cols, slot_blocks), out...]
    psum x1 -> x0, waiting for transfers between devices: 75.3 us -> none  [local(): lax.psum(jnp.where(row // per_col == col, own_window, jnp.bfloat16(0)), '...]
    dynamic_slice x3 -> x0, local copies, waits for them, and re-layouts: 16.3 us -> none  [the longest x1 13.1 us: local(): lax.dynamic_index_in_dim(cut, col, 3, keepdims=False)]
    psum x1 -> x0, blocking collectives: 12.2 us -> none  [local(): summed = lax.psum(partial_value, 'col')]
    reshape x2 -> x0, local copies, waits for them, and re-layouts: 9.39 us -> none  [the longest x1 6.42 us: local(): cut = colloc.reshape(spins, own_points, rows, cols, part)]
    unnamed x8, local copies, waits for them, and re-layouts: 1.91 us -> 10.7 us
    dot_general x1 -> x0, matrix products: 5.47 us -> none  [local(): jnp.einsum('spm,smi->spi', cut, coefficient_share, preferred_element_type...]
  transfers between devices with their start and end apart: 4 -> 0, of which waited for: 4 -> 0; matrix products, arithmetic and copies ran while one was open for 11% -> 0% of each run, Pallas kernels for 0% -> 0%
where the time goes in v2:
time: 203 us; the launch traced here: 202 us
  Pallas kernels  162 us (80%)
  matrix products  27.1 us (13%)
  local copies, waits for them, and re-layouts  11.7 us (6%)
    pallas_call x1, Pallas kernels, gathered(): pl.pallas_call(functools.partial(transfers, rows, cols, slot_blocks), out...  162 us
    dot_general x1, matrix products, local(): jnp.einsum('spm,spn->msn', basis_share, weighted, preferred_element_type=...  18.1 us
    unnamed x8, local copies, waits for them, and re-layouts  10.7 us
    dot_general x1, matrix products, local(): jnp.einsum('spq,sqn->spn', mixed_kernel, window, preferred_element_type=j...  9.04 us

profile of v2, /device:TPU:0, one launch (start us, length us, event | category | flops | bytes accessed | tf_op | source)
XLA Modules:
  0.0 202.0 jit_solution(1391134182883636250)
XLA Ops:
  0.0 1.0 slice_reduce_fusion.1
  1.0 0.7 iota_compare_fusion
  1.7 0.1 add_convert_fusion
  1.8 0.0 copy-start
  1.8 1.7 copy-done
  3.5 0.0 copy-start.1
  3.5 1.3 copy-done.1
  4.7 162.3 %shard_map.46 = (bf16[2,1024,4608]{2,1,0:T(8,128)(2,1)S(1)}, bf16[2,1024,640]{2,1,0:T(8,128)(2,1)S(1)}, bf16[2,1024,512]{2,1,0:T(8,128)(2,1)S(1)}) custom-call(bf16[2,64,9216]{2,1,0:T(8,128)(2,1)S(1)} %copy-done, bf16[2,576,512]{2,1,0:T(8,128)(2,1)S(1)} %copy-done.1), custom_call_target="tpu_custom_call" | custom-call | tf_op jit(solution)/shard_map/pallas_call | solution.py:330
  167.1 0.0 copy-start.2
  167.1 6.5 %copy-done.2 = bf16[2,1024,4608]{2,1,0:T(8,128)(2,1)} copy-done((bf16[2,1024,4608]{2,1,0:T(8,128)(2,1)}, bf16[2,1024,4608]{2,1,0:T(8,128)(2,1)S(1)}, u32[]{:S(2)}) %copy-start.2) | copy-done | bytes 18874392
  173.5 0.0 copy-start.3
  173.5 1.3 copy-done.3
  174.9 9.0 %fusion.1 = bf16[2,1024,640]{1,2,0:T(8,128)(2,1)} fusion(bf16[2,1024,640]{2,1,0:T(8,128)(2,1)S(1)} %get-tuple-element.9, f32[2,1024]{1,0:T(2,128)S(1)} %add_convert_fusion, bf16[2,1024,512]{2,1,0:T(8,128)(2,1)} %copy-done.3, pred[2,512]{1,0:T(4,128)(4,1)S(1)} %iota_compare_fusion), kind=kOutput, calls=%fused_computation.4 | convolution fusion | flops 4849664000 | bytes 7349248 | tf_op jit(solution)/shard_map/spq,sqn->spn/dot_general | solution.py:371
  183.9 18.1 %fusion = bf16[4608,2,576]{0,2,1:T(8,128)(2,1)} fusion(bf16[2,1024,4608]{2,1,0:T(8,128)(2,1)} %copy-done.2, bf16[2,1024,640]{1,2,0:T(8,128)(2,1)} %fusion.1, s32[]{:T(128)S(6)} %select_n.52), kind=kOutput, calls=%fused_computation.1 | convolution fusion | flops 10882252800 | bytes 31850500 | tf_op jit(solution)/shard_map/spm,spn->msn/dot_general | solution.py:373
  (2 shorter events, 0.0 us)
Async XLA Ops:
  1.8 1.7 copy-start
  3.5 1.3 copy-start.1
  167.1 6.5 %copy-start.2 = (bf16[2,1024,4608]{2,1,0:T(8,128)(2,1)}, bf16[2,1024,4608]{2,1,0:T(8,128)(2,1)S(1)}, u32[]{:S(2)}) copy-start(bf16[2,1024,4608]{2,1,0:T(8,128)(2,1)S(1)} %get-tuple-element.10) | copy-start | bytes 56623108
  173.5 1.3 copy-start.3

commit v3 on v2

--- a/solution.py
+++ b/solution.py
@@ -12,33 +12,28 @@
 LANES = 128
 
 
-def positions_of(offsets, points, panel_len):
-    ids = jnp.arange(points, dtype=jnp.int32)
-    first = jnp.where(ids[None, :] // panel_len == 0, offsets[:, 0:1], offsets[:, 1:2])
-    return (first + ids[None, :] % panel_len).astype(jnp.float32)
-
-
 def window_lanes(depth):
     over = LANES - math.gcd(depth, LANES)
     return -(-(depth + over) // LANES) * LANES
 
 
 class Ring:
-    def __init__(self, place, own, piece, ring_send, ring_recv, pair_send, pair_recv):
+    def __init__(self, chains, place, own, piece, ring_send, ring_recv, pair_send, pair_recv):
+        self.ways = range(2 * chains)
         self.place, self.own, self.piece = place, own, piece
         self.ring_send, self.ring_recv = ring_send, ring_recv
         self.pair_send, self.pair_recv = pair_send, pair_recv
 
     def origin(self, way, step, core):
         chips = self.place["chips"]
-        back = -step if way == 0 else step
+        back = -step if way % 2 == 0 else step
         return self.place["chip_at"](lax.rem(self.place["position"] + back + chips, chips)) * 2 + core
 
     def source(self, way, step):
         return self.own(way) if step == 0 else self.piece(way, self.origin(way, step, self.place["core"]))
 
     def hop(self, way, step):
-        target = self.place["next"] if way == 0 else self.place["previous"]
+        target = self.place["next"] if way % 2 == 0 else self.place["previous"]
         return pltpu.make_async_remote_copy(
             src_ref=self.source(way, step),
             dst_ref=self.piece(way, self.origin(way, step, self.place["core"])),
@@ -79,14 +74,14 @@
         )
 
     def begin(self):
-        for way in (0, 1):
+        for way in self.ways:
             self.hop(way, 0).start()
-        for way in (0, 1):
+        for way in self.ways:
             self.hand(way, 0).start()
 
-    def advance(self, step):
+    def advance(self, step, chain=0):
         chips = self.place["chips"]
-        for way in (0, 1):
+        for way in (2 * chain, 2 * chain + 1):
             self.landed(way, step).wait_recv()
             if step + 1 < chips - 1:
                 if step >= 1:
@@ -98,7 +93,7 @@
 
     def finish_sends(self):
         chips = self.place["chips"]
-        for way in (0, 1):
+        for way in self.ways:
             for step in range(max(chips - 3, 0), chips - 1):
                 self.hop(way, step).wait_send()
             for step in range(chips - 2, chips):
@@ -106,8 +101,8 @@
 
 
 def transfers(
-    rows, cols, slot_blocks, colloc, coefficients, basis_share, window, orbitals,
-    all_coefficients, own_colloc, own_orbitals, total, local_sem,
+    rows, cols, slot_blocks, occupied, offsets, colloc, coefficients, basis_share, window, mixed_out,
+    orbitals, mixed, all_coefficients, own_colloc, own_orbitals, total, local_sem,
     c_rs, c_rr, c_ps, c_pr, b_rs, b_rr, b_ps, b_pr, o_rs, o_rr, o_ps, o_pr,
     x_send, x_recv, w_local, y_send, y_recv,
 ):
@@ -149,19 +144,27 @@
     def point_rows(at):
         return pl.ds(pl.multiple_of(at * own_points, own_points), own_points)
 
+    sub = own_points // 2
+
+    def sub_rows(way, at):
+        return pl.ds(pl.multiple_of(at * own_points + way // 2 * sub, sub), sub)
+
     coefficient_ring = Ring(
+        1,
         place,
         lambda way: coefficients.at[spin, pl.ds(way * half, half), block_lanes],
         lambda way, at: all_coefficients.at[pl.ds(pl.multiple_of(at * depth + way * half, 16), half), :],
         c_rs, c_rr, c_ps, c_pr,
     )
     basis_ring = Ring(
+        2,
         place,
-        lambda way: colloc.at[way, :, pl.ds(share_start, share)],
-        lambda way, at: basis_share.at[way, point_rows(at), :],
+        lambda way: colloc.at[way % 2, pl.ds(way // 2 * sub, sub), pl.ds(share_start, share)],
+        lambda way, at: basis_share.at[way % 2, sub_rows(way, at), :],
         b_rs, b_rr, b_ps, b_pr,
     )
     orbital_ring = Ring(
+        1,
         place,
         lambda way: own_orbitals.at[way],
         lambda way, at: orbitals.at[way, point_rows(at), :],
@@ -192,8 +195,8 @@
     def window_piece(way, step, at_core):
         at = basis_ring.origin(way, step, at_core)
         relation = at_core_index(at_core)
-        source = basis_share.at[way, point_rows(at), pl.ds(first_lane, width)]
-        target = window.at[way, point_rows(at), :]
+        source = basis_share.at[way % 2, sub_rows(way, at), pl.ds(first_lane, width)]
+        target = window.at[way % 2, sub_rows(way, at), :]
         here = pltpu.make_async_copy(source, target, w_local.at[relation, way, step % 2])
         away = [
             pltpu.make_async_remote_copy(
@@ -211,10 +214,10 @@
 
     other_core = 1 - core
 
-    def start_window(step, at_core):
+    def start_window(step, at_core, chain):
         @pl.when(owner)
         def _():
-            for way in (0, 1):
+            for way in (2 * chain, 2 * chain + 1):
                 if step >= 2:
                     here, away = window_piece(way, step - 2, at_core)
                     here.wait()
@@ -225,18 +228,47 @@
                     copy.start()
                 here.start()
 
-    def wait_handed(ring, step):
-        for way in (0, 1):
+    def wait_handed(ring, step, chain=0):
+        for way in (2 * chain, 2 * chain + 1):
             ring.handed(way, step).wait_recv()
 
-    def basis_step(step):
-        basis_ring.advance(step)
+    def basis_step(step, chain):
+        basis_ring.advance(step, chain)
         if step == 0:
-            local[2].wait()
-            start_window(0, core)
-        start_window(step + 1, core)
-        wait_handed(basis_ring, step)
-        start_window(step, other_core)
+            if chain == 0:
+                local[2].wait()
+            start_window(0, core, chain)
+        start_window(step + 1, core, chain)
+        wait_handed(basis_ring, step, chain)
+        start_window(step, other_core, chain)
+
+    points = rows * own_points
+    panel_len = points // 2
+    screen = panel_len // 8
+    tile = LANES
+    out_copies = [
+        pltpu.make_async_copy(mixed.at[s], mixed_out.at[s], local_sem.at[4 + s]) for s in range(spins)
+    ]
+
+    def mix():
+        for s in range(spins):
+            column = lax.broadcasted_iota(jnp.int32, (1, points), 1)
+            column = jnp.where(column < panel_len, column + offsets[s, 0], column - panel_len + offsets[s, 1])
+            column = column.astype(jnp.float32)
+
+            @pl.loop(0, points // tile)
+            def _(i):
+                start = i * tile
+                panel = start // panel_len
+                line = lax.broadcasted_iota(jnp.int32, (tile, 1), 0) + (start - panel * panel_len) + offsets[s, panel]
+                distance = jnp.abs(line.astype(jnp.float32) - column)
+                at = pl.ds(pl.multiple_of(start, tile), tile)
+                density = lax.dot_general(
+                    orbitals[s, at, :], orbitals[s], (((1,), (1,)), ((), ())), preferred_element_type=jnp.float32
+                )
+                mixed[s, at, :] = (density * (screen / slots) / (screen + distance)).astype(jnp.bfloat16)
+
+            out_copies[s].start()
 
     last = chips - 1
     done = 0
@@ -244,7 +276,8 @@
     for step in range(last):
         coefficient_ring.advance(step)
         if (step + 1) * early // last > done:
-            basis_step(done)
+            basis_step(done, 0)
+            basis_step(done, 1)
             done += 1
     for step in range(chips):
         wait_handed(coefficient_ring, step)
@@ -259,7 +292,8 @@
         at = pl.ds(pl.multiple_of(i * chunk, chunk), chunk)
         total[...] += jnp.dot(own_colloc[:, at], all_coefficients[at, :], preferred_element_type=jnp.float32)
 
-    own_orbitals[spin, :, block_lanes] = total[...].astype(jnp.bfloat16)
+    slot = lax.broadcasted_iota(jnp.int32, total.shape, 1) + block * block_len
+    own_orbitals[spin, :, block_lanes] = jnp.where(slot < occupied[spin], total[...], 0.0).astype(jnp.bfloat16)
     swaps = [
         pltpu.make_async_remote_copy(
             src_ref=own_orbitals.at[spin, :, block_lanes],
@@ -285,16 +319,26 @@
     own_out.start()
     left, sent = last - done, 0
     for n in range(left):
-        basis_step(done)
+        if n == left - 1:
+            while sent < last:
+                orbital_ring.advance(sent)
+                sent += 1
+            for step in range(chips):
+                wait_handed(orbital_ring, step)
+            own_out.wait()
+            mix()
+        for chain in (0, 1):
+            basis_step(done, chain)
+            want = -(-(2 * n + chain + 1) * last // max(2 * left - 2, 1))
+            while sent < min(want, last):
+                orbital_ring.advance(sent)
+                sent += 1
         done += 1
-        while sent < last and sent < -(-(n + 1) * last // max(left - 1, 1)):
-            orbital_ring.advance(sent)
-            sent += 1
-    wait_handed(basis_ring, last)
-    start_window(last, other_core)
-    for step in range(chips):
-        wait_handed(orbital_ring, step)
-    own_out.wait()
+    for chain in (0, 1):
+        wait_handed(basis_ring, last, chain)
+        start_window(last, other_core, chain)
+    for copy in out_copies:
+        copy.wait()
     for copy in swaps:
         copy.wait_send()
     for ring in (coefficient_ring, basis_ring, orbital_ring):
@@ -304,7 +348,7 @@
     def _():
         for at_core in (core, other_core):
             for step in (last - 1, last):
-                for way in (0, 1):
+                for way in range(4):
                     here, away = window_piece(way, step, at_core)
                     here.wait()
                     for copy in away:
@@ -314,11 +358,11 @@
     def _():
         for at_core in (core, other_core):
             for step in range(chips):
-                for way in (0, 1):
+                for way in range(4):
                     window_piece(way, step, at_core)[1][0].wait_recv()
 
 
-def gathered(colloc, coefficients, rows, cols):
+def gathered(occupied, offsets, colloc, coefficients, rows, cols):
     spins, own_points, basis = colloc.shape
     depth, slots = coefficients.shape[1:]
     points, share, chips = own_points * rows, basis // cols, rows // 2
@@ -326,52 +370,70 @@
     block_len = slots // slot_blocks
     dma = pltpu.SemaphoreType.DMA
     ring = [dma((2, 2)), dma((2, chips - 1)), dma((2, 2)), dma((2, chips))]
-    anywhere = pl.BlockSpec(memory_space=pl.ANY)
+    ring_of_two = [dma((4, 2)), dma((4, chips - 1)), dma((4, 2)), dma((4, chips))]
+    hbm = pl.BlockSpec(memory_space=pltpu.HBM)
+    smem = pl.BlockSpec(memory_space=pltpu.SMEM)
     return pl.pallas_call(
         functools.partial(transfers, rows, cols, slot_blocks),
         out_shape=(
             jax.ShapeDtypeStruct((spins, points, share), colloc.dtype),
             jax.ShapeDtypeStruct((spins, points, window_lanes(depth)), colloc.dtype),
-            jax.ShapeDtypeStruct((spins, points, slots), colloc.dtype),
+            jax.ShapeDtypeStruct((spins, points, points), colloc.dtype),
         ),
-        in_specs=[anywhere] * 2,
-        out_specs=(anywhere,) * 3,
+        in_specs=[smem, smem, hbm, hbm],
+        out_specs=(hbm,) * 3,
         scratch_shapes=[
+            pltpu.VMEM((spins, points, slots), colloc.dtype),
+            pltpu.VMEM((spins, points, points), colloc.dtype),
             pltpu.VMEM((basis, block_len), colloc.dtype),
             pltpu.VMEM((own_points, basis), colloc.dtype),
             pltpu.VMEM((spins, own_points, slots), colloc.dtype),
             pltpu.VMEM((own_points, block_len), jnp.float32),
-            dma((4,)),
-            *ring, *ring, *ring,
-            dma((cols - 1, 2, 2, 2)), dma((2, 2, chips)), dma((2, 2, 2)),
+            dma((4 + spins,)),
+            *ring, *ring_of_two, *ring,
+            dma((cols - 1, 2, 4, 2)), dma((2, 4, chips)), dma((2, 4, 2)),
             dma((cols - 1,)), dma((cols - 1,)),
         ],
         compiler_params=pltpu.CompilerParams(
-            collective_id=0, has_side_effects=True, vmem_limit_bytes=24 * 2**20
+            collective_id=0, has_side_effects=True, vmem_limit_bytes=60 * 2**20
         ),
-    )(colloc, coefficients)
+    )(occupied, offsets, colloc, coefficients)
+
+
+def product(depth, scale, window, mixed, basis_share, out, whole, weighted):
+    @pl.when(pl.program_id(1) == 0)
+    def _():
+        whole[...] = lax.dot_general(
+            window[0], mixed[0], (((0,), (1,)), ((), ())), preferred_element_type=jnp.float32
+        )
+        skip = pl.multiple_of(lax.axis_index("row") * depth % LANES, math.gcd(depth, LANES))
+        weighted[...] = whole[pl.ds(skip, depth), :].astype(jnp.bfloat16)
+
+    out[0] = (jnp.dot(weighted[...], basis_share[0], preferred_element_type=jnp.float32) * scale).astype(out.dtype)
 
 
 def local(colloc, coefficients, occupied, offsets):
     rows = lax.axis_size("row")
     cols = lax.axis_size("col")
-    row = lax.axis_index("row")
-    spins, own_points, basis = colloc.shape
-    depth, slots = coefficients.shape[1:]
-    points = own_points * rows
-    panel_len = points // 2
-    screen_len = panel_len // 8
-    basis_share, window, orbitals = gathered(colloc, coefficients, rows, cols)
-    occupied_mask = jnp.arange(slots, dtype=jnp.int32)[None, :] < occupied[:, None]
-    orbitals = jnp.where(occupied_mask[:, None, :], orbitals, jnp.bfloat16(0))
-    place = positions_of(offsets, points, panel_len)
-    kernel = 1.0 / (1.0 + jnp.abs(place[:, :, None] - place[:, None, :]) / screen_len)
-    density = jnp.einsum("spi,sqi->spq", orbitals, orbitals, preferred_element_type=jnp.float32)
-    mixed_kernel = (kernel * density / slots).astype(jnp.bfloat16)
-    weighted = jnp.einsum("spq,sqn->spn", mixed_kernel, window, preferred_element_type=jnp.float32)
-    weighted = lax.dynamic_slice_in_dim(weighted.astype(jnp.bfloat16), row * depth % LANES, depth, 2)
-    result = jnp.einsum("spm,spn->msn", basis_share, weighted, preferred_element_type=jnp.float32)
-    return (result * (1.0 / math.sqrt(points))).astype(jnp.bfloat16)
+    depth = coefficients.shape[1]
+    basis_share, window, mixed = gathered(occupied, offsets, colloc, coefficients, rows, cols)
+    spins, points, share = basis_share.shape
+    width = window.shape[2]
+    tile = 9 * LANES if share % (9 * LANES) == 0 else LANES
+    result = pl.pallas_call(
+        functools.partial(product, depth, 1.0 / math.sqrt(points)),
+        out_shape=jax.ShapeDtypeStruct((spins, depth, share), colloc.dtype),
+        grid=(spins, share // tile),
+        in_specs=[
+            pl.BlockSpec((1, points, width), lambda s, m: (s, 0, 0)),
+            pl.BlockSpec((1, points, points), lambda s, m: (s, 0, 0)),
+            pl.BlockSpec((1, points, tile), lambda s, m: (s, 0, m)),
+        ],
+        out_specs=pl.BlockSpec((1, depth, tile), lambda s, m: (s, 0, m)),
+        scratch_shapes=[pltpu.VMEM((width, points), jnp.float32), pltpu.VMEM((depth, points), colloc.dtype)],
+        compiler_params=pltpu.CompilerParams(vmem_limit_bytes=60 * 2**20),
+    )(window, mixed, basis_share)
+    return jnp.transpose(result, (2, 0, 1))
 
 
 def solution(mesh):

time: 203 us -> 192 us (0.946)
  Pallas kernels: 162 us -> 191 us
  matrix products: 27.1 us -> 0 us
  local copies, waits for them, and re-layouts: 11.7 us -> 0 us
    dot_general x2 -> x0, matrix products: 27.1 us -> none  [the longest x1 18.1 us: local(): jnp.einsum('spm,spn->msn', basis_share, weighted, preferred_element_type=...]
    pallas_call x0 -> x1, Pallas kernels: none -> 23.7 us  [local(): pl.pallas_call(functools.partial(product, depth, 1.0 / math.sqrt(points))...]
    unnamed x8 -> x0, local copies, waits for them, and re-layouts: 10.7 us -> none
    pallas_call x1, Pallas kernels: 162 us -> 167 us  [gathered(): pl.pallas_call(functools.partial(transfers, rows, cols, slot_blocks), out...]
where the time goes in v3:
time: 192 us; the launch traced here: 191 us
  Pallas kernels  191 us (99%)
    pallas_call x1, Pallas kernels, gathered(): pl.pallas_call(functools.partial(transfers, rows, cols, slot_blocks), out...  167 us
    pallas_call x1, Pallas kernels, local(): pl.pallas_call(functools.partial(product, depth, 1.0 / math.sqrt(points))...  23.7 us

profile of v3, /device:TPU:0, one launch (start us, length us, event | category | flops | bytes accessed | tf_op | source)
XLA Modules:
  0.0 191.0 jit_solution(15172653383783162382)
XLA Ops:
  0.0 167.2 %shard_map.46 = (bf16[2,1024,4608]{2,1,0:T(8,128)(2,1)}, bf16[2,1024,640]{2,1,0:T(8,128)(2,1)}, bf16[2,1024,1024]{2,1,0:T(8,128)(2,1)}) custom-call(s32[2]{0:T(128)} %occupied.1, s32[2,2]{1,0:T(2,128)} %offsets.1, bf16[2,64,9216]{2,1,0:T(8,128)(2,1)} %colloc.1, bf16[2,576,512]{2,1,0:T(8,128)(2,1)} %coefficients.1), custom_call_target="tpu_custom_call" | custom-call | tf_op jit(solution)/shard_map/pallas_call | solution.py:376
  167.2 23.7 %shard_map.47 = bf16[2,576,4608]{2,1,0:T(8,128)(2,1)} custom-call(bf16[2,1024,640]{2,1,0:T(8,128)(2,1)} %get-tuple-element.8.window, bf16[2,1024,1024]{2,1,0:T(8,128)(2,1)} %get-tuple-element.9.mixed, bf16[2,1024,4608]{2,1,0:T(8,128)(2,1)} %get-tuple-element.10.basis_share), custom_call_target="tpu_custom_call" | custom-call | tf_op jit(solution)/shard_map/pallas_call | solution.py:423

commit v4 on v3

--- a/solution.py
+++ b/solution.py
@@ -245,13 +245,13 @@
     points = rows * own_points
     panel_len = points // 2
     screen = panel_len // 8
-    tile = LANES
+    tile = 2 * LANES
     out_copies = [
         pltpu.make_async_copy(mixed.at[s], mixed_out.at[s], local_sem.at[4 + s]) for s in range(spins)
     ]
 
-    def mix():
-        for s in range(spins):
+    def mix(which):
+        for s in which:
             column = lax.broadcasted_iota(jnp.int32, (1, points), 1)
             column = jnp.where(column < panel_len, column + offsets[s, 0], column - panel_len + offsets[s, 1])
             column = column.astype(jnp.float32)
@@ -318,18 +318,22 @@
     own_out = pltpu.make_async_copy(own_orbitals, orbitals.at[:, point_rows(row), :], local_sem.at[3])
     own_out.start()
     left, sent = last - done, 0
+    mixed_spins = 0
     for n in range(left):
-        if n == left - 1:
-            while sent < last:
-                orbital_ring.advance(sent)
-                sent += 1
-            for step in range(chips):
-                wait_handed(orbital_ring, step)
-            own_out.wait()
-            mix()
+        if n >= left - 2:
+            if mixed_spins == 0:
+                while sent < last:
+                    orbital_ring.advance(sent)
+                    sent += 1
+                for step in range(chips):
+                    wait_handed(orbital_ring, step)
+                own_out.wait()
+            upto = spins if n == left - 1 else spins // 2
+            mix(range(mixed_spins, upto))
+            mixed_spins = upto
         for chain in (0, 1):
             basis_step(done, chain)
-            want = -(-(2 * n + chain + 1) * last // max(2 * left - 2, 1))
+            want = -(-(2 * n + chain + 1) * last // max(2 * left - 4, 1))
             while sent < min(want, last):
                 orbital_ring.advance(sent)
                 sent += 1
@@ -419,7 +423,7 @@
     basis_share, window, mixed = gathered(occupied, offsets, colloc, coefficients, rows, cols)
     spins, points, share = basis_share.shape
     width = window.shape[2]
-    tile = 9 * LANES if share % (9 * LANES) == 0 else LANES
+    tile = next(n * LANES for n in (6, 3, 1) if share % (n * LANES) == 0)
     result = pl.pallas_call(
         functools.partial(product, depth, 1.0 / math.sqrt(points)),
         out_shape=jax.ShapeDtypeStruct((spins, depth, share), colloc.dtype),

time: 192 us -> 193 us (level)
  no operation moved by 1% of the time
where the time goes in v4:
time: 193 us; the launch traced here: 192 us
  Pallas kernels  192 us (99%)
    pallas_call x1, Pallas kernels, gathered(): pl.pallas_call(functools.partial(transfers, rows, cols, slot_blocks), out...  167 us
    pallas_call x1, Pallas kernels, local(): pl.pallas_call(functools.partial(product, depth, 1.0 / math.sqrt(points))...  24.7 us

profile of v4, /device:TPU:0, one launch (start us, length us, event | category | flops | bytes accessed | tf_op | source)
XLA Modules:
  0.0 192.2 jit_solution(2224109865812166727)
XLA Ops:
  0.0 167.5 %shard_map.46 = (bf16[2,1024,4608]{2,1,0:T(8,128)(2,1)}, bf16[2,1024,640]{2,1,0:T(8,128)(2,1)}, bf16[2,1024,1024]{2,1,0:T(8,128)(2,1)}) custom-call(s32[2]{0:T(128)} %occupied.1, s32[2,2]{1,0:T(2,128)} %offsets.1, bf16[2,64,9216]{2,1,0:T(8,128)(2,1)} %colloc.1, bf16[2,576,512]{2,1,0:T(8,128)(2,1)} %coefficients.1), custom_call_target="tpu_custom_call" | custom-call | tf_op jit(solution)/shard_map/pallas_call | solution.py:380
  167.5 24.7 %shard_map.47 = bf16[2,576,4608]{2,1,0:T(8,128)(2,1)} custom-call(bf16[2,1024,640]{2,1,0:T(8,128)(2,1)} %get-tuple-element.8.window, bf16[2,1024,1024]{2,1,0:T(8,128)(2,1)} %get-tuple-element.9.mixed, bf16[2,1024,4608]{2,1,0:T(8,128)(2,1)} %get-tuple-element.10.basis_share), custom_call_target="tpu_custom_call" | custom-call | tf_op jit(solution)/shard_map/pallas_call | solution.py:427
